TPU v7x, 32 devices: a whole 2x2x4 slice. The times are simulated.
32 devices in a mesh: parts: 2 (over y), ctx: 4 (over z), wt: 2 (over x), sub: 2 (over core).
Axes of the slice: x: 2, y: 2, z: 4, core: 2. Of those that a mesh axis runs over, the one named last changes fastest.
Arguments:
- tokens: bfloat16 [2048, 4096], P(('parts', 'ctx', 'wt')), parts along dimension 0, may hold values from -6 to 6
- block_order: int32 [32], P('parts'), parts along dimension 0, may hold values from 0 to 15, each once
- q_weight: bfloat16 [4096, 2048], P('wt', 'sub')
- key_value_weight: bfloat16 [4096, 4, 2, 128], P('wt', 'sub'), may hold values from -0.09375 to 0.09375
- out_weight: bfloat16 [2048, 4096], P('sub', 'wt'), may hold values from -0.5 to 0.5
Outputs:
- attended: bfloat16 [2048, 4096], P(('parts', 'ctx', 'wt'), 'sub'), parts along dimension 0
There are 2 independent parts, one for each index of `parts`. A program takes and returns all parts, laid end to end along the dimension named above; an argument that names none is the same for every part. Nothing has to cross between parts.
Inputs may be any that keep to these rules, and one draw needn't show every extreme that they name: block_order is a permutation of the 16 block numbers.
All inputs are finite; a program needn't handle non-finite values.
Results may differ from a plain program's by a relative error of at most 0.014.
The roundings to bfloat16 on the way count: a program that leaves them out, or rounds other values in their place, can miss the bound.
Values may be sent and summed in bfloat16 or wider, within the bound.
A program may use at most 128 MiB of HBM per device.

v0:
```python
import jax
import jax.numpy as jnp
from jax import lax
from jax.sharding import PartitionSpec as P

rope_base = 500000.0
epsilon = 1e-05


def token_positions(row_ids, block_order, block_len):
    number = block_order.shape[0]
    blocks = row_ids // block_len
    equal = blocks[:, None] == jnp.arange(number, dtype=jnp.int32)[None, :]
    chosen = jnp.sum(jnp.where(equal, block_order[None, :], 0), axis=1)
    return chosen * block_len + row_ids % block_len


def rotary(values_in, positions, head_dim):
    half_dim = head_dim // 2
    inverse_freq = rope_base ** (-(jnp.arange(half_dim, dtype=jnp.float32) * 2.0 / head_dim))
    angles = positions.astype(jnp.float32)[:, None] * inverse_freq[None, :]
    cosine = jnp.concatenate([jnp.cos(angles), jnp.cos(angles)], axis=1)[:, None, :]
    sine = jnp.concatenate([jnp.sin(angles), jnp.sin(angles)], axis=1)[:, None, :]
    rotated = jnp.concatenate([-values_in[..., half_dim:], values_in[..., :half_dim]], axis=-1)
    return values_in * cosine + rotated * sine


def body(tokens, block_order, q_weight, key_value_weight, out_weight):
    tok_rows = tokens.shape[0]
    block_len = tok_rows // 2
    head_dim = key_value_weight.shape[3]
    kv_local = key_value_weight.shape[1]
    q_cols = q_weight.shape[1]
    q_local = q_cols // head_dim
    group = q_local // kv_local
    kv_cols = kv_local * 2 * head_dim
    kv_flat = key_value_weight.reshape(key_value_weight.shape[0], kv_cols)
    own_first = lax.axis_index(("ctx", "wt")) * tok_rows
    own_ids = own_first + jnp.arange(tok_rows, dtype=jnp.int32)
    own_positions = token_positions(own_ids, block_order, block_len)
    widened = tokens.astype(jnp.float32)
    normalized_input = (
        widened * lax.rsqrt(jnp.mean(widened * widened, axis=1, keepdims=True) + epsilon)
    ).astype(jnp.bfloat16)
    queries = jnp.dot(
        normalized_input,
        lax.all_gather(q_weight, "wt", axis=0, tiled=True),
        preferred_element_type=jnp.float32,
    )
    key_value_rows = jnp.dot(
        normalized_input,
        lax.all_gather(kv_flat, "wt", axis=0, tiled=True),
        preferred_element_type=jnp.float32,
    )
    queries = queries.reshape(tok_rows, q_local, head_dim)
    key_value_rows = key_value_rows.reshape(tok_rows, kv_local, 2, head_dim)
    q_rot = rotary(queries, own_positions, head_dim).astype(jnp.bfloat16)
    k_rot = rotary(key_value_rows[:, :, 0, :], own_positions, head_dim).astype(jnp.bfloat16)
    value_rows = key_value_rows[:, :, 1, :].astype(jnp.bfloat16)
    q_grouped = jnp.transpose(q_rot.reshape(tok_rows, kv_local, group, head_dim), (1, 2, 0, 3))
    q_grouped = q_grouped.reshape(kv_local, group * tok_rows, head_dim)
    query_positions = jnp.tile(own_positions, group)
    score_factor = 1.0 / head_dim**0.5
    key_part = lax.all_gather(k_rot, ("ctx", "wt"), axis=0, tiled=True)
    value_part = lax.all_gather(value_rows, ("ctx", "wt"), axis=0, tiled=True)
    count = key_part.shape[0]
    key_ids = jnp.arange(count, dtype=jnp.int32)
    key_positions = token_positions(key_ids, block_order, block_len)
    visible = query_positions[:, None] >= key_positions[None, :]
    old_max = jnp.full((kv_local, group * tok_rows), -1e30, jnp.float32)
    scores = (
        jnp.einsum("hqd,khd->hqk", q_grouped, key_part, preferred_element_type=jnp.float32)
        * score_factor
    )
    scores = jnp.where(visible[None], scores, -1e30)
    new_max = jnp.maximum(old_max, jnp.max(scores, axis=2))
    weights = jnp.where(visible[None], jnp.exp(scores - new_max[..., None]), 0.0)
    new_total = jnp.sum(weights, axis=2)
    new_acc = jnp.einsum(
        "hqk,khd->hqd", weights.astype(jnp.bfloat16), value_part, preferred_element_type=jnp.float32
    )
    heads_out = new_acc / new_total[..., None]
    heads_out = jnp.transpose(heads_out.reshape(kv_local, group, tok_rows, head_dim), (2, 0, 1, 3))
    heads_out = heads_out.reshape(tok_rows, q_cols).astype(jnp.bfloat16)
    partial_out = jnp.dot(
        heads_out,
        lax.all_gather(out_weight, "wt", axis=1, tiled=True),
        preferred_element_type=jnp.float32,
    )
    return lax.psum_scatter(
        partial_out.astype(jnp.bfloat16), "sub", scatter_dimension=1, tiled=True
    )


def solution(mesh):
    in_specs = (
        P(("parts", "ctx", "wt"), None),
        P("parts"),
        P("wt", "sub"),
        P("wt", "sub", None, None),
        P("sub", "wt"),
    )
    out_specs = P(("parts", "ctx", "wt"), "sub")
    return jax.shard_map(body, mesh=mesh, in_specs=in_specs, out_specs=out_specs, check_vma=False)
```

profile of v0, /device:TPU:1, one launch (start us, length us, event | category | flops | bytes accessed | tf_op | source)
XLA Modules:
  0.0 318.7 jit_solution(17308050258334250507)
XLA Ops:
  6.5 4.1 %reshape.158 = bf16[2048,512]{1,0:T(8,128)(2,1)} reshape(bf16[2048,2,2,128]{3,2,1,0:T(2,128)(2,1)} %param.8) | data formatting | bytes 4194304 | tf_op jit(solution)/shard_map/reshape | solution.py:37
  10.7 0.0 all-gather.5.cloned.1.call-start
  10.7 0.7 all-gather.5.cloned.1.call-update
  11.5 0.7 all-gather.9.cloned.1.call-update
  12.3 0.1 select_reduce_fusion.1
  12.4 0.1 select_reduce_fusion
  12.5 0.3 multiply_cosine_fusion
  12.8 0.1 pad_maximum_fusion
  12.9 0.3 fusion.3
  13.2 0.4 broadcast_compare_fusion
  13.6 56.1 %all-gather.7.cloned.1.call-done = bf16[4096,512]{1,0:T(8,128)(2,1)} async-done(((bf16[2048,512]{1,0:T(8,128)(2,1)}), bf16[4096,512]{1,0:T(8,128)(2,1)}) %all-gather.7.cloned.1.call-update) | async-done | bytes 4194320 | tf_op jit(solution)/shard_map/all_gather | solution.py:52
  69.7 2.9 fusion.17
  72.6 0.2 reshape.159
  72.8 0.1 slice.27
  72.9 0.1 slice.30
  73.1 0.1 slice_negate_fusion.1
  73.2 0.1 fusion.23
  73.3 25.7 %all_gather.17 = bf16[1024,2,128]{2,0,1:T(8,128)(2,1)S(1)} all-gather(bf16[128,2,128]{2,0,1:T(8,128)(2,1)S(1)} %fusion.23), channel_id=1, replica_groups=mesh['parts'=2,'ctx'=4,'wt'=2,'sub'=2] {'ctx','wt'}, dimensions={0}, use_global_device_ids=true | all-gather | bytes 589824 | tf_op jit(solution)/shard_map/all_gather | solution.py:64
  99.0 25.9 %all-gather = bf16[1024,2,1,128]{3,0,1,2:T(8,128)(2,1)S(1)} all-gather(bf16[128,2,1,128]{3,0,1,2:T(8,128)(2,1)S(1)} %copy.24), channel_id=2, replica_groups=mesh['parts'=2,'ctx'=4,'wt'=2,'sub'=2] {'ctx','wt'}, dimensions={0}, use_global_device_ids=true | all-gather | bytes 589824 | tf_op jit(solution)/shard_map/all_gather | solution.py:65
  124.9 67.4 %all-gather.5.cloned.1.call-done = bf16[4096,1024]{1,0:T(8,128)(2,1)} async-done(((bf16[2048,1024]{1,0:T(8,128)(2,1)}), bf16[4096,1024]{1,0:T(8,128)(2,1)}) %all-gather.5.cloned.1.call-update) | async-done | bytes 8388624 | tf_op jit(solution)/shard_map/all_gather | solution.py:47
  192.3 4.7 %fusion.19 = f32[128,1024]{1,0:T(8,128)S(1)} fusion(bf16[4096,1024]{1,0:T(8,128)(2,1)} %all-gather.5.cloned.1.call-done, bf16[128,4096]{1,0:T(8,128)(2,1)S(1)} %copy-done, f32[128]{0:T(128)S(1)} %add_rsqrt_fusion), kind=kOutput, calls=%fused_computation.21 | convolution fusion | flops 1075314688 | bytes 9961984 | tf_op jit(solution)/shard_map/dot_general | solution.py:45
  197.0 0.2 reshape.155
  197.2 0.1 copy.19
  197.3 0.2 slice_negate_fusion
  197.6 0.4 fusion.21
  198.0 1.1 fusion
  199.1 1.5 fusion.1
  200.5 1.6 fusion.11
  202.1 0.2 copy.16
  202.3 95.0 %all-gather.9.cloned.1.call-done = bf16[1024,4096]{1,0:T(8,128)(2,1)} async-done(((bf16[1024,2048]{1,0:T(8,128)(2,1)}), bf16[1024,4096]{1,0:T(8,128)(2,1)}) %all-gather.9.cloned.1.call-update) | async-done | bytes 8388624 | tf_op jit(solution)/shard_map/all_gather | solution.py:87
  297.3 5.7 %convolution_convert_fusion = bf16[128,4096]{1,0:T(8,128)(2,1)} fusion(bf16[128,1024]{0,1:T(8,128)(2,1)S(1)} %bitcast.31, bf16[1024,4096]{1,0:T(8,128)(2,1)} %all-gather.9.cloned.1.call-done), kind=kOutput, calls=%fused_computation | convolution fusion | flops 1074266112 | bytes 9699328 | tf_op jit(solution)/shard_map/dot_general | solution.py:85
  303.1 9.1 %reduce-scatter.2.cloned.1.call-done = bf16[128,2048]{1,0:T(8,128)(2,1)} async-done(((bf16[128,4096]{1,0:T(8,128)(2,1)}), bf16[128,2048]{1,0:T(8,128)(2,1)}) %reduce-scatter.2.cloned.1.call-update) | async-done | bytes 524304 | tf_op jit(solution)/shard_map/reduce_scatter | solution.py:90
  (20 shorter events, 0.3 us)
Async XLA Ops:
  6.5 63.1 %all-gather.7.cloned.1.call-start = ((), (), s32[]{:S(2)}) async-start(), calls=%async_computation.2 | async-start | bytes 6291456 | tf_op jit(solution)/shard_map/all_gather | solution.py:52
  10.7 1.6 copy-start.1
  10.7 2.2 copy-start
  10.7 181.6 %all-gather.5.cloned.1.call-start = ((), (), s32[]{:S(2)}) async-start(), calls=%async_computation.1 | async-start | bytes 12582912 | tf_op jit(solution)/shard_map/all_gather | solution.py:47
  11.4 285.9 %all-gather.9.cloned.1.call-start = ((), (), s32[]{:S(2)}) async-start(), calls=%async_computation.3 | async-start | bytes 12582912 | tf_op jit(solution)/shard_map/all_gather | solution.py:87
  12.2 299.9 %reduce-scatter.2.cloned.1.call-start = ((), (), s32[]{:S(2)}) async-start(), calls=%async_computation.4 | async-start | bytes 1572864 | tf_op jit(solution)/shard_map/reduce_scatter | solution.py:90
Sparse Core Ops, SparseCore 0:
  10.8 58.8 all-gather.6
  71.2 121.0 all-gather.4
  193.9 103.4 all-gather.8
  303.2 8.8 reduce-scatter.1
where the time goes:
time: 319 us
  waiting for transfers between devices  229 us (72%)
  blocking collectives  51.6 us (16%)
  matrix products  16 us (5%)
  between operations  13.4 us (4%)
  local copies, waits for them, and re-layouts  5.11 us (2%)
  other arithmetic  3.57 us (1%)
    all_gather x1, waiting for transfers between devices, body(): lax.all_gather(out_weight, 'wt', axis=1, tiled=True)  95 us
    all_gather x1, waiting for transfers between devices, body(): lax.all_gather(q_weight, 'wt', axis=0, tiled=True)  67.4 us
    all_gather x1, waiting for transfers between devices, body(): lax.all_gather(kv_flat, 'wt', axis=0, tiled=True)  56.1 us
    all_gather x1, blocking collectives, body(): value_part = lax.all_gather(value_rows, ('ctx', 'wt'), axis=0, tiled=True)  25.9 us
    all_gather x1, blocking collectives, body(): key_part = lax.all_gather(k_rot, ('ctx', 'wt'), axis=0, tiled=True)  25.7 us
    reduce_scatter x1, waiting for transfers between devices, body(): lax.psum_scatter(partial_out.astype(jnp.bfloat16), 'sub', scatter_dimensi...  9.05 us
  transfers between devices with their start and end apart: 4, of which 4 were waited for; matrix products, arithmetic and copies ran while one was open for 5% of the time, Pallas kernels for 0%

commit v1 on v0

--- a/solution.py
+++ b/solution.py
@@ -1,7 +1,13 @@
+import functools
+
 import jax
 import jax.numpy as jnp
 from jax import lax
+from jax.experimental import pallas as pl
+from jax.experimental.pallas import tpu as pltpu
 from jax.sharding import PartitionSpec as P
+
+MESH = pl.DeviceIdType.MESH
 
 rope_base = 500000.0
 epsilon = 1e-05
@@ -92,6 +98,456 @@
     )
 
 
+OUT_CHUNKS = 4
+ROW_CHUNKS = 2
+
+
+def fused_kernel(
+    n,
+    tokens,
+    cosine,
+    sine,
+    q_pos,
+    k_pos,
+    q_hbm,
+    kv_hbm,
+    o_hbm,
+    out,
+    q_w,
+    kv_raw,
+    kv_wide,
+    kv_w,
+    o_w,
+    x_own,
+    x_send,
+    x_recv,
+    pkv_send,
+    pkv_recv,
+    pq_send,
+    pq_recv,
+    kv_keep,
+    q_keep,
+    q_rot,
+    kv_all,
+    heads,
+    o_keep,
+    o_send,
+    o_recv,
+    o_fin,
+    o_last,
+    load_sem,
+    xs_sem,
+    xr_sem,
+    fs_sem,
+    fr_sem,
+    ps_sem,
+    pr_sem,
+    zs_sem,
+    zr_sem,
+    hs_sem,
+    hr_sem,
+    os_sem,
+    or_sem,
+    ls_sem,
+    lr_sem,
+):
+    c = lax.axis_index("ctx")
+    w = lax.axis_index("wt")
+    s = lax.axis_index("sub")
+    rows, width = tokens.shape
+    feats = width // 2
+    part = feats // 2
+    hd = 128
+    q_half = q_w.shape[2]
+    heads_here = q_half // hd
+    partner = {"wt": 1 - w}
+    sibling = {"sub": 1 - s}
+    across = {"wt": 1 - w, "sub": 1 - s}
+
+    loads = [
+        pltpu.make_async_copy(kv_hbm, kv_raw, load_sem.at[0]),
+        pltpu.make_async_copy(
+            q_hbm.at[:, pl.ds(pl.multiple_of((1 - w) * q_half, q_half), q_half)],
+            q_w.at[0],
+            load_sem.at[1],
+        ),
+        pltpu.make_async_copy(
+            q_hbm.at[:, pl.ds(pl.multiple_of(w * q_half, q_half), q_half)],
+            q_w.at[1],
+            load_sem.at[2],
+        ),
+        pltpu.make_async_copy(o_hbm, o_w, load_sem.at[3]),
+    ]
+    for load in loads:
+        load.start()
+
+    barrier = pltpu.get_barrier_semaphore()
+    for target in (partner, sibling, across):
+        pl.semaphore_signal(barrier, inc=1, device_id=target, device_id_type=MESH)
+
+    @pl.when(c > 0)
+    def _():
+        pl.semaphore_signal(barrier, inc=1, device_id={"ctx": c - 1}, device_id_type=MESH)
+
+    @pl.when(c < n - 1)
+    def _():
+        pl.semaphore_signal(barrier, inc=1, device_id={"ctx": c + 1}, device_id_type=MESH)
+
+    step = 16
+    chunk = rows // ROW_CHUNKS
+    own_at = pl.multiple_of(w * feats, feats)
+    send_at = pl.multiple_of((1 - w) * feats + s * part, part)
+
+    def normalise(i, carry):
+        at = pl.ds(pl.multiple_of(i * step, step), step)
+        whole = tokens[at, :].astype(jnp.float32)
+        scale = lax.rsqrt(jnp.mean(whole * whole, axis=1, keepdims=True) + epsilon)
+        x_send[at, :] = (tokens[at, pl.ds(send_at, part)].astype(jnp.float32) * scale).astype(
+            jnp.bfloat16
+        )
+        x_own[at, :] = (tokens[at, pl.ds(own_at, feats)].astype(jnp.float32) * scale).astype(
+            jnp.bfloat16
+        )
+        return carry
+
+    x_copies = []
+    for j in range(ROW_CHUNKS):
+        lax.fori_loop(j * (chunk // step), (j + 1) * (chunk // step), normalise, 0)
+        if j == 0:
+            pl.semaphore_wait(
+                barrier, 3 + jnp.minimum(c, 1) + jnp.minimum(n - 1 - c, 1)
+            )
+
+        copy = pltpu.make_async_remote_copy(
+            src_ref=x_send.at[pl.ds(j * chunk, chunk)],
+            dst_ref=x_recv.at[s, pl.ds(j * chunk, chunk)],
+            send_sem=xs_sem.at[j],
+            recv_sem=xr_sem.at[j],
+            device_id=partner,
+            device_id_type=MESH,
+        )
+        copy.start()
+        x_copies.append(copy)
+
+    loads[0].wait()
+    kv_wide[...] = kv_raw[...].astype(jnp.float32)
+    for h in range(2):
+        for t in range(2):
+            kv_w[h, :, t * hd : (t + 1) * hd] = kv_wide[
+                pl.ds(h * 2 + t, feats, stride=4), :
+            ].astype(jnp.bfloat16)
+
+    def send_part(index, src, dst, block):
+        copy = pltpu.make_async_remote_copy(
+            src_ref=src.at[block],
+            dst_ref=dst.at[block],
+            send_sem=ps_sem.at[index],
+            recv_sem=pr_sem.at[index],
+            device_id=partner,
+            device_id_type=MESH,
+        )
+        copy.start()
+        return copy
+
+    f32 = jnp.float32
+    own = x_own[...]
+    pkv_send[w] = jnp.dot(own, kv_w[1 - w], preferred_element_type=f32).astype(jnp.bfloat16)
+    parts = [send_part(0, pkv_send, pkv_recv, w)]
+    loads[1].wait()
+    pq_send[w] = jnp.dot(own, q_w[0], preferred_element_type=f32).astype(jnp.bfloat16)
+    parts.append(send_part(1, pq_send, pq_recv, w))
+
+    forwards = []
+    for j in range(ROW_CHUNKS):
+        x_copies[j].wait_recv()
+        copy = pltpu.make_async_remote_copy(
+            src_ref=x_recv.at[s, pl.ds(j * chunk, chunk)],
+            dst_ref=x_recv.at[s, pl.ds(j * chunk, chunk)],
+            send_sem=fs_sem.at[j],
+            recv_sem=fr_sem.at[j],
+            device_id=sibling,
+            device_id_type=MESH,
+        )
+        copy.start()
+        forwards.append(copy)
+    kv_keep[w] = jnp.dot(own, kv_w[w], preferred_element_type=f32)
+    for copy in forwards:
+        copy.wait()
+
+    def other(weight):
+        return jnp.dot(x_recv[0], weight[:part], preferred_element_type=f32) + jnp.dot(
+            x_recv[1], weight[part:], preferred_element_type=f32
+        )
+
+    pkv_send[1 - w] = other(kv_w[1 - w]).astype(jnp.bfloat16)
+    parts.append(send_part(2, pkv_send, pkv_recv, 1 - w))
+    pq_send[1 - w] = other(q_w[0]).astype(jnp.bfloat16)
+    parts.append(send_part(3, pq_send, pq_recv, 1 - w))
+    kv_keep[1 - w] = other(kv_w[w])
+
+    def rotate(t, block):
+        turned = pltpu.roll(t, hd // 2, 1)
+        return (t * cosine[block] + turned * sine[block]).astype(jnp.bfloat16)
+
+    def z_copy(way, t, b):
+        block = c - t if way == 0 else c + t
+        at = pl.ds(pl.multiple_of(block * 2 * rows + b * rows, rows), rows)
+        return pltpu.make_async_remote_copy(
+            src_ref=kv_all.at[at],
+            dst_ref=kv_all.at[at],
+            send_sem=zs_sem.at[way, t, b],
+            recv_sem=zr_sem.at[way, t, b],
+            device_id={"ctx": c + 1 if way == 0 else c - 1},
+            device_id_type=MESH,
+        )
+
+    def z_sends(way, t):
+        if way == 0:
+            return jnp.logical_and(c - t >= 0, c < n - 1)
+        return jnp.logical_and(c + t <= n - 1, c > 0)
+
+    def z_gets(way, t):
+        return c - 1 - t >= 0 if way == 0 else c + 1 + t <= n - 1
+
+    for order, index in ((1, 0), (0, 2)):
+        parts[index].wait_recv()
+        b = jnp.where(order == 0, w, 1 - w)
+        kv = kv_keep[b] + pkv_recv[b].astype(f32)
+        at = pl.ds(pl.multiple_of(c * 2 * rows + b * rows, rows), rows)
+        kv_all[at, :hd] = rotate(kv[:, :hd], b)
+        kv_all[at, hd:] = kv[:, hd:].astype(jnp.bfloat16)
+        for way in range(2):
+
+            @pl.when(z_sends(way, 0))
+            def _():
+                z_copy(way, 0, b).start()
+
+    loads[2].wait()
+    q_keep[w] = jnp.dot(own, q_w[1], preferred_element_type=f32)
+    q_keep[1 - w] = other(q_w[1])
+
+    for t in range(n - 1):
+        for order in (1, 0):
+            b = jnp.where(order == 0, w, 1 - w)
+            for way in range(2):
+
+                @pl.when(z_gets(way, t))
+                def _():
+                    z_copy(way, t, b).wait_recv()
+
+                if t < n - 2:
+
+                    @pl.when(z_sends(way, t + 1))
+                    def _():
+                        z_copy(way, t + 1, b).start()
+
+    for order, index in ((1, 1), (0, 3)):
+        parts[index].wait_recv()
+        b = jnp.where(order == 0, w, 1 - w)
+        q = q_keep[b] + pq_recv[b].astype(f32)
+        at = pl.ds(pl.multiple_of(b * rows, rows), rows)
+        for h in range(heads_here):
+            q_rot[h, at, :] = rotate(q[:, h * hd : (h + 1) * hd], b)
+
+    h_copies = []
+    factor = 1.0 / hd**0.5
+    for h in range(heads_here):
+        visible = q_pos[...] >= k_pos[...]
+        scores = (
+            lax.dot_general(
+                q_rot[h], kv_all[:, :hd], (((1,), (1,)), ((), ())), preferred_element_type=f32
+            )
+            * factor
+        )
+        scores = jnp.where(visible, scores, -1e30)
+        top = jnp.max(scores, axis=1, keepdims=True)
+        weights = jnp.where(visible, jnp.exp(scores - top), 0.0)
+        total = jnp.sum(weights, axis=1, keepdims=True)
+        mixed = jnp.dot(weights.astype(jnp.bfloat16), kv_all[:, hd:], preferred_element_type=f32)
+        heads[w, h // 2, :, (h % 2) * hd : (h % 2 + 1) * hd] = (mixed / total).astype(jnp.bfloat16)
+        place = heads.at[w, h // 2, :, pl.ds((h % 2) * hd, hd)]
+        copy = pltpu.make_async_remote_copy(
+            src_ref=place,
+            dst_ref=place,
+            send_sem=hs_sem.at[h],
+            recv_sem=hr_sem.at[h],
+            device_id=partner,
+            device_id_type=MESH,
+        )
+        copy.start()
+        h_copies.append(copy)
+    loads[3].wait()
+    for copy in h_copies:
+        copy.wait_recv()
+
+    span = o_w.shape[1] // OUT_CHUNKS
+
+    def project(block, j):
+        at = pl.ds(pl.multiple_of(block * rows, rows), rows)
+        total = None
+        for g in range(2):
+            for p in range(heads_here // 2):
+                first = (g * (heads_here // 2) + p) * 2 * hd
+                term = jnp.dot(
+                    heads[g, p, at, :],
+                    o_w[first : first + 2 * hd, j * span : (j + 1) * span],
+                    preferred_element_type=f32,
+                )
+                total = term if total is None else total + term
+        return total
+
+    def o_copy(j):
+        return pltpu.make_async_remote_copy(
+            src_ref=o_send.at[j],
+            dst_ref=o_recv.at[j],
+            send_sem=os_sem.at[j],
+            recv_sem=or_sem.at[j],
+            device_id=sibling,
+            device_id_type=MESH,
+        )
+
+    def last_copy(j):
+        return pltpu.make_async_remote_copy(
+            src_ref=o_fin.at[j],
+            dst_ref=o_last.at[j],
+            send_sem=ls_sem.at[j],
+            recv_sem=lr_sem.at[j],
+            device_id=across,
+            device_id_type=MESH,
+        )
+
+    for j in range(OUT_CHUNKS):
+        o_keep[...] = project(1 - w, j)
+
+        @pl.when(s == w)
+        def _():
+            o_send[j] = o_keep[...].astype(jnp.bfloat16)
+            o_copy(j).start()
+
+        @pl.when(s != w)
+        def _():
+            o_copy(j).wait_recv()
+            o_fin[j] = (o_keep[...] + o_recv[j].astype(f32)).astype(jnp.bfloat16)
+            last_copy(j).start()
+
+    for j in range(OUT_CHUNKS):
+        o_keep[...] = project(w, j)
+
+        @pl.when(s != w)
+        def _():
+            o_send[j] = o_keep[...].astype(jnp.bfloat16)
+            o_copy(j).start()
+
+        @pl.when(s == w)
+        def _():
+            o_copy(j).wait_recv()
+            out[:, j * span : (j + 1) * span] = (o_keep[...] + o_recv[j].astype(f32)).astype(
+                jnp.bfloat16
+            )
+
+    for j in range(OUT_CHUNKS):
+
+        @pl.when(s != w)
+        def _():
+            last_copy(j).wait()
+            out[:, j * span : (j + 1) * span] = o_last[j]
+
+        o_copy(j).wait_send()
+
+    for copy in x_copies + parts + h_copies:
+        copy.wait_send()
+    for t in range(n - 1):
+        for order in (1, 0):
+            b = jnp.where(order == 0, w, 1 - w)
+            for way in range(2):
+
+                @pl.when(z_sends(way, t))
+                def _():
+                    z_copy(way, t, b).wait_send()
+
+
+def fused_body(n, tokens, block_order, q_weight, key_value_weight, out_weight):
+    rows, width = tokens.shape
+    feats, kv_local, _, hd = key_value_weight.shape
+    q_half = q_weight.shape[1] // 2
+    block_len = rows // 2
+    first = lax.axis_index("ctx") * 2 * rows
+    own_positions = token_positions(
+        first + jnp.arange(2 * rows, dtype=jnp.int32), block_order, block_len
+    )
+    key_positions = token_positions(
+        jnp.arange(2 * rows * n, dtype=jnp.int32), block_order, block_len
+    )
+    half = hd // 2
+    inverse_freq = rope_base ** (-(jnp.arange(half, dtype=jnp.float32) * 2.0 / hd))
+    angles = own_positions.astype(jnp.float32)[:, None] * inverse_freq[None, :]
+    cosine = jnp.concatenate([jnp.cos(angles), jnp.cos(angles)], axis=1).reshape(2, rows, hd)
+    sine = jnp.concatenate([-jnp.sin(angles), jnp.sin(angles)], axis=1).reshape(2, rows, hd)
+    bf16, f32 = jnp.bfloat16, jnp.float32
+    span = out_weight.shape[1] // OUT_CHUNKS
+    here = q_half // hd
+    dma = pltpu.SemaphoreType.DMA
+    vmem = pl.BlockSpec(memory_space=pltpu.VMEM)
+    hbm = pl.BlockSpec(memory_space=pl.ANY)
+    return pl.pallas_call(
+        functools.partial(fused_kernel, n),
+        out_shape=jax.ShapeDtypeStruct((rows, out_weight.shape[1]), bf16),
+        in_specs=[vmem] * 5 + [hbm] * 3,
+        out_specs=vmem,
+        scratch_shapes=[
+            pltpu.VMEM((2, feats, q_half), bf16),
+            pltpu.VMEM((feats * kv_local * 2, hd), bf16),
+            pltpu.VMEM((feats * kv_local * 2, hd), f32),
+            pltpu.VMEM((2, feats, 2 * hd), bf16),
+            pltpu.VMEM(out_weight.shape, bf16),
+            pltpu.VMEM((rows, feats), bf16),
+            pltpu.VMEM((rows, feats // 2), bf16),
+            pltpu.VMEM((2, rows, feats // 2), bf16),
+            pltpu.VMEM((2, rows, 2 * hd), bf16),
+            pltpu.VMEM((2, rows, 2 * hd), bf16),
+            pltpu.VMEM((2, rows, q_half), bf16),
+            pltpu.VMEM((2, rows, q_half), bf16),
+            pltpu.VMEM((2, rows, 2 * hd), f32),
+            pltpu.VMEM((2, rows, q_half), f32),
+            pltpu.VMEM((here, 2 * rows, hd), bf16),
+            pltpu.VMEM((n * 2 * rows, 2 * hd), bf16),
+            pltpu.VMEM((2, here // 2, 2 * rows, 2 * hd), bf16),
+            pltpu.VMEM((rows, span), f32),
+            pltpu.VMEM((OUT_CHUNKS, rows, span), bf16),
+            pltpu.VMEM((OUT_CHUNKS, rows, span), bf16),
+            pltpu.VMEM((OUT_CHUNKS, rows, span), bf16),
+            pltpu.VMEM((OUT_CHUNKS, rows, span), bf16),
+            dma((4,)),
+            dma((ROW_CHUNKS,)),
+            dma((ROW_CHUNKS,)),
+            dma((ROW_CHUNKS,)),
+            dma((ROW_CHUNKS,)),
+            dma((4,)),
+            dma((4,)),
+            dma((2, n - 1, 2)),
+            dma((2, n - 1, 2)),
+            dma((here,)),
+            dma((here,)),
+            dma((OUT_CHUNKS,)),
+            dma((OUT_CHUNKS,)),
+            dma((OUT_CHUNKS,)),
+            dma((OUT_CHUNKS,)),
+        ],
+        compiler_params=pltpu.CompilerParams(
+            collective_id=0, has_side_effects=True, vmem_limit_bytes=56 * 1024 * 1024
+        ),
+    )(
+        tokens,
+        cosine,
+        sine,
+        own_positions[:, None],
+        key_positions[None, :],
+        q_weight,
+        key_value_weight.reshape(feats * kv_local * 2, hd),
+        out_weight,
+    )
+
+
 def solution(mesh):
     in_specs = (
         P(("parts", "ctx", "wt"), None),
@@ -101,4 +557,7 @@
         P("sub", "wt"),
     )
     out_specs = P(("parts", "ctx", "wt"), "sub")
-    return jax.shard_map(body, mesh=mesh, in_specs=in_specs, out_specs=out_specs, check_vma=False)
+    n = mesh.shape["ctx"]
+    fits = mesh.shape["wt"] == 2 and mesh.shape["sub"] == 2 and 1 < n <= 8
+    run = functools.partial(fused_body, n) if fits else body
+    return jax.shard_map(run, mesh=mesh, in_specs=in_specs, out_specs=out_specs, check_vma=False)

time: 319 us -> 52 us (0.16)
  waiting for transfers between devices: 229 us -> 0 us
  blocking collectives: 51.6 us -> 0 us
  Pallas kernels: 0 us -> 45.5 us
  matrix products: 16 us -> 0 us
  between operations: 13.4 us -> 0.05 us
    all_gather x3 -> x0, waiting for transfers between devices: 219 us -> none  [the longest x1 95 us: body(): lax.all_gather(out_weight, 'wt', axis=1, tiled=True)]
    all_gather x2 -> x0, blocking collectives: 51.6 us -> none  [the longest x1 25.9 us: body(): value_part = lax.all_gather(value_rows, ('ctx', 'wt'), axis=0, tiled=True)]
    pallas_call x0 -> x1, Pallas kernels: none -> 45.5 us  [fused_body(): pl.pallas_call(functools.partial(fused_kernel, n), out_shape=jax.ShapeDty...]
    dot_general x5 -> x0, matrix products: 16 us -> none  [the longest x1 5.72 us: body(): jnp.dot(heads_out, lax.all_gather(out_weight, 'wt', axis=1, tiled=True),...]
    reduce_scatter x1 -> x0, waiting for transfers between devices: 9.05 us -> none  [body(): lax.psum_scatter(partial_out.astype(jnp.bfloat16), 'sub', scatter_dimensi...]
    reshape x3 -> x0, local copies, waits for them, and re-layouts: 4.53 us -> none  [the longest x1 4.11 us: body(): kv_flat = key_value_weight.reshape(key_value_weight.shape[0], kv_cols)]
  transfers between devices with their start and end apart: 4 -> 0, of which waited for: 4 -> 0; matrix products, arithmetic and copies ran while one was open for 5% -> 0% of each run, Pallas kernels for 0% -> 0%
where the time goes in v1:
time: 52 us; the launch traced here: 51.8 us
  Pallas kernels  45.5 us (88%)
  other arithmetic  4.2 us (8%)
  local copies, waits for them, and re-layouts  2.01 us (4%)
    pallas_call x1, Pallas kernels, fused_body(): pl.pallas_call(functools.partial(fused_kernel, n), out_shape=jax.ShapeDty...  45.5 us
    unnamed x1, local copies, waits for them, and re-layouts  1.88 us
    reduce_sum x2, other arithmetic, token_positions(): chosen = jnp.sum(jnp.where(equal, block_order[None, :], 0), axis=1)  1.48 us
    add x2, other arithmetic, token_positions(): return chosen * block_len + row_ids % block_len  1.3 us

profile of v1, /device:TPU:1, one launch (start us, length us, event | category | flops | bytes accessed | tf_op | source)
XLA Modules:
  0.0 51.8 jit_solution(16263166068775757385)
XLA Ops:
  0.0 0.7 %select_reduce_fusion.1 = s32[256]{0:T(256)S(1)} fusion(s32[16]{0:T(128)} %param.6, s32[256]{0:T(256)S(1)} %and_select_fusion.2), kind=kLoop, calls=%fused_computation.15 | loop fusion | flops 12032 | bytes 2112 | tf_op jit(solution)/shard_map/reduce_sum | solution.py:20
  0.8 0.7 %select_reduce_fusion = s32[1024]{0:T(1024)S(1)} fusion(s32[16]{0:T(128)} %param.6, s32[1024]{0:T(1024)S(1)} %add_select_fusion.1), kind=kLoop, calls=%fused_computation.12 | loop fusion | flops 48128 | bytes 8256 | tf_op jit(solution)/shard_map/reduce_sum | solution.py:20
  1.6 0.6 %fusion.6.k_pos = s32[1,1024]{1,0:T(1,128)} fusion(s32[1,1024]{1,0:T(1,128)S(1)} %bitcast.8), kind=kLoop, calls=%fused_computation.22 | loop fusion | flops 7168 | bytes 8192 | tf_op jit(solution)/shard_map/add | solution.py:21
  2.2 0.1 copy.7
  2.3 0.7 %fusion.1.q_pos = s32[256,1]{1,0:T(8,128)} fusion(s32[256,1]{1,0:T(8,128)S(1)} %copy.7, s32[]{:T(128)S(6)} %mul.58), kind=kLoop, calls=%fused_computation.6 | loop fusion | flops 3328 | bytes 2052 | tf_op jit(solution)/shard_map/add | solution.py:21
  3.0 0.5 %fusion.5 = (f32[2,128,64]{2,1,0:T(8,128)S(1)}, f32[2,128,64]{2,1,0:T(8,128)S(1)}, f32[2,128,64]{2,1,0:T(8,128)S(1)}) fusion(f32[64]{0:T(128)S(1)} %negate_power_fusion, f32[2,128]{1,0:T(2,128)S(1)} %fusion.12), kind=kLoop, calls=%fused_computation.14 | loop fusion | flops 32768 | bytes 197888 | tf_op jit(solution)/shard_map/neg | solution.py:485
  3.5 0.8 %pad_maximum_fusion = (f32[2,128,128]{2,1,0:T(8,128)}, f32[2,128,128]{2,1,0:T(8,128)}) fusion(f32[2,128,64]{2,1,0:T(8,128)S(1)} %get-tuple-element.7, f32[2,128,64]{2,1,0:T(8,128)S(1)} %get-tuple-element.6, f32[2,128,64]{2,1,0:T(8,128)S(1)} %get-tuple-element.5), kind=kLoop, calls=%fused_computation.7 | loop fusion | flops 65536 | bytes 458752 | tf_op jit(solution)/shard_map/concatenate | solution.py:484
  4.4 45.5 %shard_map.55 = bf16[128,2048]{1,0:T(8,128)(2,1)} custom-call(bf16[128,4096]{1,0:T(8,128)(2,1)} %tokens.1, f32[2,128,128]{2,1,0:T(8,128)} %get-tuple-element.8.cosine, f32[2,128,128]{2,1,0:T(8,128)} %get-tuple-element.9.sine, s32[256,1]{1,0:T(8,128)} %fusion.1.q_pos, s32[1,1024]{1,0:T(1,128)} %fusion.6.k_pos, bf16[2048,1024]{1,0:T(8,128)(2,1)} %q_hbm.1, ...), custom_call_target="tpu_custom_call" | custom-call | tf_op jit(solution)/shard_map/pallas_call | solution.py:492
  49.9 1.9 %copy.9 = bf16[128,2048]{1,0:T(8,128)(2,1)} copy(bf16[128,2048]{1,0:T(8,128)(2,1)} %shard_map.55) | data formatting | bytes 1048576
  (6 shorter events, 0.0 us)

commit v2 on v1

--- a/solution.py
+++ b/solution.py
@@ -2,6 +2,7 @@
 
 import jax
 import jax.numpy as jnp
+import numpy as np
 from jax import lax
 from jax.experimental import pallas as pl
 from jax.experimental.pallas import tpu as pltpu
@@ -99,20 +100,21 @@
 
 
 OUT_CHUNKS = 4
-ROW_CHUNKS = 2
+ROW_CHUNKS = 4
 
 
 def fused_kernel(
     n,
-    tokens,
-    cosine,
-    sine,
-    q_pos,
-    k_pos,
+    token_hbm,
+    order,
+    freq,
     q_hbm,
     kv_hbm,
     o_hbm,
     out,
+    tokens,
+    cosine,
+    sine,
     q_w,
     kv_raw,
     kv_wide,
@@ -135,6 +137,7 @@
     o_recv,
     o_fin,
     o_last,
+    token_sem,
     load_sem,
     xs_sem,
     xr_sem,
@@ -164,6 +167,17 @@
     sibling = {"sub": 1 - s}
     across = {"wt": 1 - w, "sub": 1 - s}
 
+    chunk = rows // ROW_CHUNKS
+    token_loads = [
+        pltpu.make_async_copy(
+            token_hbm.at[pl.ds(j * chunk, chunk)],
+            tokens.at[pl.ds(j * chunk, chunk)],
+            token_sem.at[j],
+        )
+        for j in range(ROW_CHUNKS)
+    ]
+    for load in token_loads:
+        load.start()
     loads = [
         pltpu.make_async_copy(kv_hbm, kv_raw, load_sem.at[0]),
         pltpu.make_async_copy(
@@ -194,7 +208,6 @@
         pl.semaphore_signal(barrier, inc=1, device_id={"ctx": c + 1}, device_id_type=MESH)
 
     step = 16
-    chunk = rows // ROW_CHUNKS
     own_at = pl.multiple_of(w * feats, feats)
     send_at = pl.multiple_of((1 - w) * feats + s * part, part)
 
@@ -212,6 +225,7 @@
 
     x_copies = []
     for j in range(ROW_CHUNKS):
+        token_loads[j].wait()
         lax.fori_loop(j * (chunk // step), (j + 1) * (chunk // step), normalise, 0)
         if j == 0:
             pl.semaphore_wait(
@@ -228,6 +242,39 @@
         )
         copy.start()
         x_copies.append(copy)
+
+    forwards = []
+
+    def forward(j):
+        x_copies[j].wait_recv()
+        copy = pltpu.make_async_remote_copy(
+            src_ref=x_recv.at[s, pl.ds(j * chunk, chunk)],
+            dst_ref=x_recv.at[s, pl.ds(j * chunk, chunk)],
+            send_sem=fs_sem.at[j],
+            recv_sem=fr_sem.at[j],
+            device_id=sibling,
+            device_id_type=MESH,
+        )
+        copy.start()
+        forwards.append(copy)
+
+    block_len = rows // 2
+    q_row = lax.broadcasted_iota(jnp.int32, (2 * rows, 1), 0)
+    q_pos = q_row % block_len
+    for k in range(4):
+        here = q_row // block_len == k
+        q_pos = q_pos + jnp.where(here, order[c * 4 + k] * block_len, 0)
+    k_col = lax.broadcasted_iota(jnp.int32, (1, 2 * rows * n), 1)
+    k_pos = k_col % block_len
+    for k in range(4 * n):
+        k_pos = k_pos + jnp.where(k_col // block_len == k, order[k] * block_len, 0)
+    low = lax.broadcasted_iota(jnp.int32, (rows, hd), 1) < hd // 2
+    for b in range(2):
+        angles = q_pos[b * rows : (b + 1) * rows].astype(jnp.float32) * freq[...]
+        cosine[b] = jnp.cos(angles)
+        turn = jnp.sin(angles)
+        sine[b] = jnp.where(low, -turn, turn)
+    forward(0)
 
     loads[0].wait()
     kv_wide[...] = kv_raw[...].astype(jnp.float32)
@@ -236,6 +283,7 @@
             kv_w[h, :, t * hd : (t + 1) * hd] = kv_wide[
                 pl.ds(h * 2 + t, feats, stride=4), :
             ].astype(jnp.bfloat16)
+    forward(1)
 
     def send_part(index, src, dst, block):
         copy = pltpu.make_async_remote_copy(
@@ -252,25 +300,14 @@
     f32 = jnp.float32
     own = x_own[...]
     pkv_send[w] = jnp.dot(own, kv_w[1 - w], preferred_element_type=f32).astype(jnp.bfloat16)
-    parts = [send_part(0, pkv_send, pkv_recv, w)]
+    kv_keep[w] = jnp.dot(own, kv_w[w], preferred_element_type=f32)
+    forward(2)
     loads[1].wait()
     pq_send[w] = jnp.dot(own, q_w[0], preferred_element_type=f32).astype(jnp.bfloat16)
-    parts.append(send_part(1, pq_send, pq_recv, w))
-
-    forwards = []
-    for j in range(ROW_CHUNKS):
-        x_copies[j].wait_recv()
-        copy = pltpu.make_async_remote_copy(
-            src_ref=x_recv.at[s, pl.ds(j * chunk, chunk)],
-            dst_ref=x_recv.at[s, pl.ds(j * chunk, chunk)],
-            send_sem=fs_sem.at[j],
-            recv_sem=fr_sem.at[j],
-            device_id=sibling,
-            device_id_type=MESH,
-        )
-        copy.start()
-        forwards.append(copy)
-    kv_keep[w] = jnp.dot(own, kv_w[w], preferred_element_type=f32)
+    forward(3)
+    for copy in x_copies:
+        copy.wait_send()
+    parts = [send_part(0, pkv_send, pkv_recv, w)]
     for copy in forwards:
         copy.wait()
 
@@ -280,9 +317,7 @@
         )
 
     pkv_send[1 - w] = other(kv_w[1 - w]).astype(jnp.bfloat16)
-    parts.append(send_part(2, pkv_send, pkv_recv, 1 - w))
-    pq_send[1 - w] = other(q_w[0]).astype(jnp.bfloat16)
-    parts.append(send_part(3, pq_send, pq_recv, 1 - w))
+    parts.append(send_part(1, pkv_send, pkv_recv, 1 - w))
     kv_keep[1 - w] = other(kv_w[w])
 
     def rotate(t, block):
@@ -309,9 +344,8 @@
     def z_gets(way, t):
         return c - 1 - t >= 0 if way == 0 else c + 1 + t <= n - 1
 
-    for order, index in ((1, 0), (0, 2)):
+    for b, index in ((1 - w, 0), (w, 1)):
         parts[index].wait_recv()
-        b = jnp.where(order == 0, w, 1 - w)
         kv = kv_keep[b] + pkv_recv[b].astype(f32)
         at = pl.ds(pl.multiple_of(c * 2 * rows + b * rows, rows), rows)
         kv_all[at, :hd] = rotate(kv[:, :hd], b)
@@ -322,13 +356,15 @@
             def _():
                 z_copy(way, 0, b).start()
 
+    parts.append(send_part(2, pq_send, pq_recv, w))
+    pq_send[1 - w] = other(q_w[0]).astype(jnp.bfloat16)
+    parts.append(send_part(3, pq_send, pq_recv, 1 - w))
     loads[2].wait()
     q_keep[w] = jnp.dot(own, q_w[1], preferred_element_type=f32)
     q_keep[1 - w] = other(q_w[1])
 
     for t in range(n - 1):
-        for order in (1, 0):
-            b = jnp.where(order == 0, w, 1 - w)
+        for b in (1 - w, w):
             for way in range(2):
 
                 @pl.when(z_gets(way, t))
@@ -341,9 +377,8 @@
                     def _():
                         z_copy(way, t + 1, b).start()
 
-    for order, index in ((1, 1), (0, 3)):
+    for b, index in ((1 - w, 2), (w, 3)):
         parts[index].wait_recv()
-        b = jnp.where(order == 0, w, 1 - w)
         q = q_keep[b] + pq_recv[b].astype(f32)
         at = pl.ds(pl.multiple_of(b * rows, rows), rows)
         for h in range(heads_here):
@@ -352,7 +387,7 @@
     h_copies = []
     factor = 1.0 / hd**0.5
     for h in range(heads_here):
-        visible = q_pos[...] >= k_pos[...]
+        visible = q_pos >= k_pos
         scores = (
             lax.dot_general(
                 q_rot[h], kv_all[:, :hd], (((1,), (1,)), ((), ())), preferred_element_type=f32
@@ -454,11 +489,10 @@
 
         o_copy(j).wait_send()
 
-    for copy in x_copies + parts + h_copies:
+    for copy in parts + h_copies:
         copy.wait_send()
     for t in range(n - 1):
-        for order in (1, 0):
-            b = jnp.where(order == 0, w, 1 - w)
+        for b in (1 - w, w):
             for way in range(2):
 
                 @pl.when(z_sends(way, t))
@@ -471,30 +505,24 @@
     feats, kv_local, _, hd = key_value_weight.shape
     q_half = q_weight.shape[1] // 2
     block_len = rows // 2
-    first = lax.axis_index("ctx") * 2 * rows
-    own_positions = token_positions(
-        first + jnp.arange(2 * rows, dtype=jnp.int32), block_order, block_len
-    )
-    key_positions = token_positions(
-        jnp.arange(2 * rows * n, dtype=jnp.int32), block_order, block_len
-    )
-    half = hd // 2
-    inverse_freq = rope_base ** (-(jnp.arange(half, dtype=jnp.float32) * 2.0 / hd))
-    angles = own_positions.astype(jnp.float32)[:, None] * inverse_freq[None, :]
-    cosine = jnp.concatenate([jnp.cos(angles), jnp.cos(angles)], axis=1).reshape(2, rows, hd)
-    sine = jnp.concatenate([-jnp.sin(angles), jnp.sin(angles)], axis=1).reshape(2, rows, hd)
+    steps = np.arange(hd // 2) * 2.0 / hd
+    freq = np.tile(rope_base ** (-steps), 2)[None].astype(np.float32)
     bf16, f32 = jnp.bfloat16, jnp.float32
     span = out_weight.shape[1] // OUT_CHUNKS
     here = q_half // hd
     dma = pltpu.SemaphoreType.DMA
     vmem = pl.BlockSpec(memory_space=pltpu.VMEM)
+    smem = pl.BlockSpec(memory_space=pltpu.SMEM)
     hbm = pl.BlockSpec(memory_space=pl.ANY)
     return pl.pallas_call(
         functools.partial(fused_kernel, n),
         out_shape=jax.ShapeDtypeStruct((rows, out_weight.shape[1]), bf16),
-        in_specs=[vmem] * 5 + [hbm] * 3,
+        in_specs=[hbm, smem, vmem] + [hbm] * 3,
         out_specs=vmem,
         scratch_shapes=[
+            pltpu.VMEM(tokens.shape, bf16),
+            pltpu.VMEM((2, rows, hd), f32),
+            pltpu.VMEM((2, rows, hd), f32),
             pltpu.VMEM((2, feats, q_half), bf16),
             pltpu.VMEM((feats * kv_local * 2, hd), bf16),
             pltpu.VMEM((feats * kv_local * 2, hd), f32),
@@ -517,6 +545,7 @@
             pltpu.VMEM((OUT_CHUNKS, rows, span), bf16),
             pltpu.VMEM((OUT_CHUNKS, rows, span), bf16),
             pltpu.VMEM((OUT_CHUNKS, rows, span), bf16),
+            dma((ROW_CHUNKS,)),
             dma((4,)),
             dma((ROW_CHUNKS,)),
             dma((ROW_CHUNKS,)),
@@ -538,10 +567,8 @@
         ),
     )(
         tokens,
-        cosine,
-        sine,
-        own_positions[:, None],
-        key_positions[None, :],
+        block_order,
+        jnp.asarray(freq),
         q_weight,
         key_value_weight.reshape(feats * kv_local * 2, hd),
         out_weight,

time: 52 us -> 46.8 us (0.90)
  other arithmetic: 4.2 us -> 0 us
  Pallas kernels: 45.5 us -> 44.7 us
    reduce_sum x2 -> x0, other arithmetic: 1.48 us -> none  [token_positions(): chosen = jnp.sum(jnp.where(equal, block_order[None, :], 0), axis=1)]
    add x2 -> x0, other arithmetic: 1.3 us -> none  [token_positions(): return chosen * block_len + row_ids % block_len]
    concatenate x1 -> x0, other arithmetic: 0.84 us -> none  [fused_body(): jnp.concatenate([jnp.cos(angles), jnp.cos(angles)], axis=1)]
    pallas_call x1, Pallas kernels: 45.5 us -> 44.7 us  [fused_body(): pl.pallas_call(functools.partial(fused_kernel, n), out_shape=jax.ShapeDty...]
    neg x1 -> x0, other arithmetic: 0.53 us -> none  [fused_body(): -jnp.sin(angles)]
where the time goes in v2:
time: 46.8 us; the launch traced here: 46.6 us
  Pallas kernels  44.7 us (96%)
  local copies, waits for them, and re-layouts  1.88 us (4%)
    pallas_call x1, Pallas kernels, fused_body(): pl.pallas_call(functools.partial(fused_kernel, n), out_shape=jax.ShapeDty...  44.7 us
    unnamed x1, local copies, waits for them, and re-layouts  1.88 us

profile of v2, /device:TPU:1, one launch (start us, length us, event | category | flops | bytes accessed | tf_op | source)
XLA Modules:
  0.0 46.6 jit_solution(9517727539866881463)
XLA Ops:
  0.0 44.7 %shard_map.64 = bf16[128,2048]{1,0:T(8,128)(2,1)} custom-call(bf16[128,4096]{1,0:T(8,128)(2,1)} %token_hbm.1, s32[16]{0:T(128)} %order.1, f32[1,128]{1,0:T(1,128)} %constant.2.clone.freq, bf16[2048,1024]{1,0:T(8,128)(2,1)} %q_hbm.1, bf16[8192,128]{1,0:T(8,128)(2,1)} %bitcast.1, bf16[1024,2048]{1,0:T(8,128)(2,1)} %o_hbm.1), custom_call_target="tpu_custom_call" | custom-call | tf_op jit(solution)/shard_map/pallas_call | solution.py:517
  44.7 1.9 %copy.8 = bf16[128,2048]{1,0:T(8,128)(2,1)} copy(bf16[128,2048]{1,0:T(8,128)(2,1)} %shard_map.64) | data formatting | bytes 1048576

commit v3 on v2

--- a/solution.py
+++ b/solution.py
@@ -199,13 +199,16 @@
     for target in (partner, sibling, across):
         pl.semaphore_signal(barrier, inc=1, device_id=target, device_id_type=MESH)
 
-    @pl.when(c > 0)
-    def _():
-        pl.semaphore_signal(barrier, inc=1, device_id={"ctx": c - 1}, device_id_type=MESH)
-
-    @pl.when(c < n - 1)
-    def _():
-        pl.semaphore_signal(barrier, inc=1, device_id={"ctx": c + 1}, device_id_type=MESH)
+    reach = min(2, n - 1)
+    for d in range(1, reach + 1):
+
+        @pl.when(c >= d)
+        def _():
+            pl.semaphore_signal(barrier, inc=1, device_id={"ctx": c - d}, device_id_type=MESH)
+
+        @pl.when(c < n - d)
+        def _():
+            pl.semaphore_signal(barrier, inc=1, device_id={"ctx": c + d}, device_id_type=MESH)
 
     step = 16
     own_at = pl.multiple_of(w * feats, feats)
@@ -229,7 +232,7 @@
         lax.fori_loop(j * (chunk // step), (j + 1) * (chunk // step), normalise, 0)
         if j == 0:
             pl.semaphore_wait(
-                barrier, 3 + jnp.minimum(c, 1) + jnp.minimum(n - 1 - c, 1)
+                barrier, 3 + jnp.minimum(c, reach) + jnp.minimum(n - 1 - c, reach)
             )
 
         copy = pltpu.make_async_remote_copy(
@@ -324,25 +327,38 @@
         turned = pltpu.roll(t, hd // 2, 1)
         return (t * cosine[block] + turned * sine[block]).astype(jnp.bfloat16)
 
-    def z_copy(way, t, b):
-        block = c - t if way == 0 else c + t
+    def z_copy(way, d, b):
+        sign = 1 - 2 * way
+        block = c if d < 3 else c - 2 * sign
         at = pl.ds(pl.multiple_of(block * 2 * rows + b * rows, rows), rows)
         return pltpu.make_async_remote_copy(
             src_ref=kv_all.at[at],
             dst_ref=kv_all.at[at],
-            send_sem=zs_sem.at[way, t, b],
-            recv_sem=zr_sem.at[way, t, b],
-            device_id={"ctx": c + 1 if way == 0 else c - 1},
+            send_sem=zs_sem.at[way, d - 1, b],
+            recv_sem=zr_sem.at[way, d - 1, b],
+            device_id={"ctx": c + sign * (d if d < 3 else 1)},
             device_id_type=MESH,
         )
 
-    def z_sends(way, t):
+    def z_sends(way, d):
+        if d < 3:
+            return c < n - d if way == 0 else c >= d
         if way == 0:
-            return jnp.logical_and(c - t >= 0, c < n - 1)
-        return jnp.logical_and(c + t <= n - 1, c > 0)
-
-    def z_gets(way, t):
-        return c - 1 - t >= 0 if way == 0 else c + 1 + t <= n - 1
+            return jnp.logical_and(c >= 2, c < n - 1)
+        return jnp.logical_and(c < n - 2, c > 0)
+
+    def z_gets(way, d):
+        return c >= d if way == 0 else c < n - d
+
+    def z_get(way, d, b):
+        @pl.when(z_gets(way, d))
+        def _():
+            z_copy(way, d, b).wait_recv()
+
+    def z_send(way, d, b):
+        @pl.when(z_sends(way, d))
+        def _():
+            z_copy(way, d, b).start()
 
     for b, index in ((1 - w, 0), (w, 1)):
         parts[index].wait_recv()
@@ -350,11 +366,9 @@
         at = pl.ds(pl.multiple_of(c * 2 * rows + b * rows, rows), rows)
         kv_all[at, :hd] = rotate(kv[:, :hd], b)
         kv_all[at, hd:] = kv[:, hd:].astype(jnp.bfloat16)
-        for way in range(2):
-
-            @pl.when(z_sends(way, 0))
-            def _():
-                z_copy(way, 0, b).start()
+        for d in range(reach, 0, -1):
+            for way in range(2):
+                z_send(way, d, b)
 
     parts.append(send_part(2, pq_send, pq_recv, w))
     pq_send[1 - w] = other(q_w[0]).astype(jnp.bfloat16)
@@ -363,19 +377,12 @@
     q_keep[w] = jnp.dot(own, q_w[1], preferred_element_type=f32)
     q_keep[1 - w] = other(q_w[1])
 
-    for t in range(n - 1):
+    if n > 2:
         for b in (1 - w, w):
             for way in range(2):
-
-                @pl.when(z_gets(way, t))
-                def _():
-                    z_copy(way, t, b).wait_recv()
-
-                if t < n - 2:
-
-                    @pl.when(z_sends(way, t + 1))
-                    def _():
-                        z_copy(way, t + 1, b).start()
+                z_get(way, 2, b)
+                if n > 3:
+                    z_send(way, 3, b)
 
     for b, index in ((1 - w, 2), (w, 3)):
         parts[index].wait_recv()
@@ -383,6 +390,12 @@
         at = pl.ds(pl.multiple_of(b * rows, rows), rows)
         for h in range(heads_here):
             q_rot[h, at, :] = rotate(q[:, h * hd : (h + 1) * hd], b)
+
+    for d in (1, 3):
+        if d < n:
+            for b in (1 - w, w):
+                for way in range(2):
+                    z_get(way, d, b)
 
     h_copies = []
     factor = 1.0 / hd**0.5
@@ -491,13 +504,13 @@
 
     for copy in parts + h_copies:
         copy.wait_send()
-    for t in range(n - 1):
+    for d in range(1, n):
         for b in (1 - w, w):
             for way in range(2):
 
-                @pl.when(z_sends(way, t))
+                @pl.when(z_sends(way, d))
                 def _():
-                    z_copy(way, t, b).wait_send()
+                    z_copy(way, d, b).wait_send()
 
 
 def fused_body(n, tokens, block_order, q_weight, key_value_weight, out_weight):
@@ -585,6 +598,6 @@
     )
     out_specs = P(("parts", "ctx", "wt"), "sub")
     n = mesh.shape["ctx"]
-    fits = mesh.shape["wt"] == 2 and mesh.shape["sub"] == 2 and 1 < n <= 8
+    fits = mesh.shape["wt"] == 2 and mesh.shape["sub"] == 2 and 1 < n <= 4
     run = functools.partial(fused_body, n) if fits else body
     return jax.shard_map(run, mesh=mesh, in_specs=in_specs, out_specs=out_specs, check_vma=False)

time: 46.8 us -> 44.6 us (0.953)
  Pallas kernels: 44.7 us -> 42.5 us
    pallas_call x1, Pallas kernels: 44.7 us -> 42.5 us  [fused_body(): pl.pallas_call(functools.partial(fused_kernel, n), out_shape=jax.ShapeDty...]
where the time goes in v3:
time: 44.6 us; the launch traced here: 44.4 us
  Pallas kernels  42.5 us (95%)
  local copies, waits for them, and re-layouts  1.88 us (4%)
    pallas_call x1, Pallas kernels, fused_body(): pl.pallas_call(functools.partial(fused_kernel, n), out_shape=jax.ShapeDty...  42.5 us
    unnamed x1, local copies, waits for them, and re-layouts  1.88 us

profile of v3, /device:TPU:1, one launch (start us, length us, event | category | flops | bytes accessed | tf_op | source)
XLA Modules:
  0.0 44.4 jit_solution(1594619892550173547)
XLA Ops:
  0.0 42.5 %shard_map.64 = bf16[128,2048]{1,0:T(8,128)(2,1)} custom-call(bf16[128,4096]{1,0:T(8,128)(2,1)} %token_hbm.1, s32[16]{0:T(128)} %order.1, f32[1,128]{1,0:T(1,128)} %constant.2.clone.freq, bf16[2048,1024]{1,0:T(8,128)(2,1)} %q_hbm.1, bf16[8192,128]{1,0:T(8,128)(2,1)} %bitcast.1, bf16[1024,2048]{1,0:T(8,128)(2,1)} %o_hbm.1), custom_call_target="tpu_custom_call" | custom-call | tf_op jit(solution)/shard_map/pallas_call | solution.py:530
  42.5 1.9 %copy.8 = bf16[128,2048]{1,0:T(8,128)(2,1)} copy(bf16[128,2048]{1,0:T(8,128)(2,1)} %shard_map.64) | data formatting | bytes 1048576

commit v4 on v3

--- a/solution.py
+++ b/solution.py
@@ -322,6 +322,7 @@
     pkv_send[1 - w] = other(kv_w[1 - w]).astype(jnp.bfloat16)
     parts.append(send_part(1, pkv_send, pkv_recv, 1 - w))
     kv_keep[1 - w] = other(kv_w[w])
+    parts.append(send_part(2, pq_send, pq_recv, w))
 
     def rotate(t, block):
         turned = pltpu.roll(t, hd // 2, 1)
@@ -370,7 +371,6 @@
             for way in range(2):
                 z_send(way, d, b)
 
-    parts.append(send_part(2, pq_send, pq_recv, w))
     pq_send[1 - w] = other(q_w[0]).astype(jnp.bfloat16)
     parts.append(send_part(3, pq_send, pq_recv, 1 - w))
     loads[2].wait()

time: 44.6 us -> 44.6 us (level)
  no operation moved by 1% of the time
where the time goes in v4:
time: 44.6 us; the launch traced here: 44.4 us
  Pallas kernels  42.5 us (95%)
  local copies, waits for them, and re-layouts  1.88 us (4%)
    pallas_call x1, Pallas kernels, fused_body(): pl.pallas_call(functools.partial(fused_kernel, n), out_shape=jax.ShapeDty...  42.5 us
    unnamed x1, local copies, waits for them, and re-layouts  1.88 us

profile of v4, /device:TPU:1, one launch (start us, length us, event | category | flops | bytes accessed | tf_op | source)
XLA Modules:
  0.0 44.4 jit_solution(17991795291352273694)
XLA Ops:
  0.0 42.5 %shard_map.64 = bf16[128,2048]{1,0:T(8,128)(2,1)} custom-call(bf16[128,4096]{1,0:T(8,128)(2,1)} %token_hbm.1, s32[16]{0:T(128)} %order.1, f32[1,128]{1,0:T(1,128)} %constant.2.clone.freq, bf16[2048,1024]{1,0:T(8,128)(2,1)} %q_hbm.1, bf16[8192,128]{1,0:T(8,128)(2,1)} %bitcast.1, bf16[1024,2048]{1,0:T(8,128)(2,1)} %o_hbm.1), custom_call_target="tpu_custom_call" | custom-call | tf_op jit(solution)/shard_map/pallas_call | solution.py:530
  42.5 1.9 %copy.8 = bf16[128,2048]{1,0:T(8,128)(2,1)} copy(bf16[128,2048]{1,0:T(8,128)(2,1)} %shard_map.64) | data formatting | bytes 1048576
